TPU v7x, 256 devices: a whole 4x4x8 slice. The times are simulated.
256 devices in a mesh: dp: 32 (over y, z), cent: 8 (over x, core).
Axes of the slice: x: 4, y: 4, z: 8, core: 2. Of those that a mesh axis runs over, the one named last changes fastest.
Arguments:
- stream: bfloat16 [65536, 768], P('dp'), may hold values from -6 to 6
- sample_index: int32 [32768], P('dp'), may hold values from 0 to 2047
- centroids: float32 [16384, 768], P(('cent', 'dp')), may hold values from -6 to 6
- first_moment: float32 [16384, 768], P(('cent', 'dp')), may hold values from -3 to 3
- second_moment: float32 [16384, 768], P(('cent', 'dp')), may hold values from 0.01 to 1
Outputs:
- new_centroids: float32 [16384, 768], P(('cent', 'dp'))
- new_first: float32 [16384, 768], P(('cent', 'dp'))
- new_second: float32 [16384, 768], P(('cent', 'dp'))
All inputs are finite; a program needn't handle non-finite values.
Results may differ from a plain program's by a relative error of at most 0.0003.
Values may be sent and summed in bfloat16 or wider, within the bound.
A program may use at most 64 MiB of HBM per device.

v0:
```python
import math
import jax
import jax.numpy as jnp
from jax import lax
from jax.sharding import PartitionSpec as P

KB = 16384
ITERS = 3
temper = 2.0
beta_one = 0.9
beta_two = 0.99
step_rate = 0.05
epsilon = 1e-08


def per_device(stream, sample_index, centroids, first_moment, second_moment):
    embedded = stream[sample_index]
    local_rows = embedded.shape[0]
    total_rows = local_rows * lax.axis_size("dp")
    balance = math.log(total_rows / KB)
    rounded = centroids.astype(jnp.bfloat16)
    shard_piece = lax.all_gather(rounded, "dp", axis=0, tiled=True)
    squares = jnp.sum(shard_piece.astype(jnp.float32) ** 2, axis=1)
    product = lax.dot_general(
        embedded, shard_piece, (((1,), (1,)), ((), ())), preferred_element_type=jnp.float32
    )
    logits = (2.0 * product - squares[None, :]) / temper

    def row_potential(column_pot):
        shifted = logits + column_pot[None, :]
        highest = jnp.max(shifted, axis=1)
        summed = jnp.sum(jnp.exp(shifted - highest[:, None]), axis=1)
        overall = lax.pmax(highest, "cent")
        summed = lax.psum(summed * jnp.exp(highest - overall), "cent")
        highest = overall
        return -(highest + jnp.log(summed))

    column_pot = jnp.zeros((logits.shape[1],), jnp.float32)
    for sweep_index in range(ITERS):
        column_shifted = logits + row_potential(column_pot)[:, None]
        column_highest = jnp.max(column_shifted, axis=0)
        column_summed = jnp.sum(jnp.exp(column_shifted - column_highest[None, :]), axis=0)
        column_overall = lax.pmax(column_highest, "dp")
        column_summed = lax.psum(column_summed * jnp.exp(column_highest - column_overall), "dp")
        column_highest = column_overall
        column_pot = balance - (column_highest + jnp.log(column_summed))
    row_pot = row_potential(column_pot)
    transport = jnp.exp(logits + row_pot[:, None] + column_pot[None, :]).astype(jnp.bfloat16)
    weighted = lax.dot_general(
        transport, embedded, (((0,), (0,)), ((), ())), preferred_element_type=jnp.float32
    )
    weight_mass = jnp.sum(transport.astype(jnp.float32), axis=0)
    weighted, weight_mass = lax.psum((weighted, weight_mass), "dp")
    owned_rows = centroids.shape[0]
    offset_rows = lax.axis_index("dp") * owned_rows
    weighted = lax.dynamic_slice_in_dim(weighted, offset_rows, owned_rows, 0)
    weight_mass = lax.dynamic_slice_in_dim(weight_mass, offset_rows, owned_rows, 0)
    gradient = (weight_mass[:, None] * centroids - weighted) * (KB / total_rows)
    new_first = beta_one * first_moment + (1.0 - beta_one) * gradient
    new_second = beta_two * second_moment + (1.0 - beta_two) * gradient * gradient
    new_centroids = centroids - step_rate * new_first / (jnp.sqrt(new_second) + epsilon)
    return (new_centroids, new_first, new_second)


def solution(mesh):
    return jax.shard_map(
        per_device,
        mesh=mesh,
        in_specs=(
            P("dp", None),
            P("dp"),
            P(("cent", "dp"), None),
            P(("cent", "dp"), None),
            P(("cent", "dp"), None),
        ),
        out_specs=(P(("cent", "dp"), None), P(("cent", "dp"), None), P(("cent", "dp"), None)),
        check_vma=False,
    )
```

profile of v0, /device:TPU:1, one launch (start us, length us, event | category | flops | bytes accessed | tf_op | source)
XLA Modules:
  0.0 889.1 jit_solution(12046903474257052355)
XLA Ops:
  9.7 5.2 gather_fusion
  15.0 76.0 %all-gather.2.cloned.1.call-done = bf16[2048,768]{1,0:T(8,128)(2,1)} async-done(((bf16[64,768]{1,0:T(8,128)(2,1)}), bf16[2048,768]{1,0:T(8,128)(2,1)}) %all-gather.2.cloned.1.call-update) | async-done | bytes 3145744 | tf_op jit(solution)/shard_map/all_gather | solution.py:22
  93.6 9.1 %fusion.2 = (f32[1024]{0:T(1024)S(1)}, f32[1024,2048]{1,0:T(8,128)}) fusion(f32[2048]{0:T(1024)S(1)} %multiply_reduce_fusion, bf16[1024,768]{1,0:T(8,128)(2,1)} %gather_fusion, bf16[2048,768]{1,0:T(8,128)(2,1)} %all-gather.2.cloned.1.call-done), kind=kOutput, calls=%fused_computation.39 | convolution fusion | flops 3229613056 | bytes 13119488 | tf_op jit(solution)/shard_map/dot_general | solution.py:24
  102.6 16.4 %pmax.49 = f32[1024]{0:T(1024)S(1)} all-reduce(f32[1024]{0:T(1024)S(1)} %get-tuple-element.6), channel_id=1, replica_groups=mesh['dp'=32,'cent'=8] {'cent'}, use_global_device_ids=true, to_apply=%region_2.0 | all-reduce | flops 1024 | bytes 8192 | tf_op jit(solution)/shard_map/pmax | solution.py:33
  119.0 4.6 exponential_reduce_fusion.6
  123.6 12.4 %psum.63 = f32[1024]{0:T(1024)S(1)} all-reduce(f32[1024]{0:T(1024)S(1)} %exponential_multiply_fusion.6), channel_id=1, replica_groups=mesh['dp'=32,'cent'=8] {'cent'}, use_global_device_ids=true, to_apply=%region_4.0 | all-reduce | flops 1024 | bytes 8192 | tf_op jit(solution)/shard_map/psum | solution.py:34
  140.1 4.3 exponential_reduce_fusion.5
  144.4 58.9 %pmax.50 = f32[2048]{0:T(1024)S(1)} all-reduce(f32[2048]{0:T(1024)S(1)} %add_reduce_fusion.5), channel_id=1, replica_groups=mesh['dp'=32,'cent'=8] {'dp'}, use_global_device_ids=true, to_apply=%region_6.0 | all-reduce | flops 2048 | bytes 16384 | tf_op jit(solution)/shard_map/pmax | solution.py:43
  203.3 56.7 %psum.64 = f32[2048]{0:T(1024)S(1)} all-reduce(f32[2048]{0:T(1024)S(1)} %exponential_multiply_fusion.2), channel_id=1, replica_groups=mesh['dp'=32,'cent'=8] {'dp'}, use_global_device_ids=true, to_apply=%region_8.0 | all-reduce | flops 2048 | bytes 16384 | tf_op jit(solution)/shard_map/psum | solution.py:44
  260.1 4.0 add_reduce_fusion.4
  264.1 4.4 exponential_reduce_fusion.4
  268.5 40.3 %pmax.51 = f32[1024]{0:T(1024)S(1)} all-reduce(f32[1024]{0:T(1024)S(1)} %add_reduce_fusion.4), channel_id=1, replica_groups=mesh['dp'=32,'cent'=8] {'cent'}, use_global_device_ids=true, to_apply=%region_10.0 | all-reduce | flops 1024 | bytes 8192 | tf_op jit(solution)/shard_map/pmax | solution.py:33
  308.8 12.4 %psum.65 = f32[1024]{0:T(1024)S(1)} all-reduce(f32[1024]{0:T(1024)S(1)} %exponential_multiply_fusion.5), channel_id=1, replica_groups=mesh['dp'=32,'cent'=8] {'cent'}, use_global_device_ids=true, to_apply=%region_12.0 | all-reduce | flops 1024 | bytes 8192 | tf_op jit(solution)/shard_map/psum | solution.py:34
  321.2 4.0 add_reduce_fusion.3
  325.3 4.3 exponential_reduce_fusion.3
  329.6 59.1 %pmax.52 = f32[2048]{0:T(1024)S(1)} all-reduce(f32[2048]{0:T(1024)S(1)} %add_reduce_fusion.3), channel_id=1, replica_groups=mesh['dp'=32,'cent'=8] {'dp'}, use_global_device_ids=true, to_apply=%region_14.0 | all-reduce | flops 2048 | bytes 16384 | tf_op jit(solution)/shard_map/pmax | solution.py:43
  388.7 57.2 %psum.66 = f32[2048]{0:T(1024)S(1)} all-reduce(f32[2048]{0:T(1024)S(1)} %exponential_multiply_fusion.1), channel_id=1, replica_groups=mesh['dp'=32,'cent'=8] {'dp'}, use_global_device_ids=true, to_apply=%region_16.0 | all-reduce | flops 2048 | bytes 16384 | tf_op jit(solution)/shard_map/psum | solution.py:44
  446.0 4.0 add_reduce_fusion.2
  450.0 4.4 exponential_reduce_fusion.2
  454.4 39.6 %pmax.53 = f32[1024]{0:T(1024)S(1)} all-reduce(f32[1024]{0:T(1024)S(1)} %add_reduce_fusion.2), channel_id=1, replica_groups=mesh['dp'=32,'cent'=8] {'cent'}, use_global_device_ids=true, to_apply=%region_18.0 | all-reduce | flops 1024 | bytes 8192 | tf_op jit(solution)/shard_map/pmax | solution.py:33
  494.0 12.4 %psum.67 = f32[1024]{0:T(1024)S(1)} all-reduce(f32[1024]{0:T(1024)S(1)} %exponential_multiply_fusion.4), channel_id=1, replica_groups=mesh['dp'=32,'cent'=8] {'cent'}, use_global_device_ids=true, to_apply=%region_20.0 | all-reduce | flops 1024 | bytes 8192 | tf_op jit(solution)/shard_map/psum | solution.py:34
  506.4 4.0 add_reduce_fusion.1
  510.4 4.3 exponential_reduce_fusion.1
  514.7 59.2 %pmax.54 = f32[2048]{0:T(1024)S(1)} all-reduce(f32[2048]{0:T(1024)S(1)} %add_reduce_fusion.1), channel_id=1, replica_groups=mesh['dp'=32,'cent'=8] {'dp'}, use_global_device_ids=true, to_apply=%region_22.0 | all-reduce | flops 2048 | bytes 16384 | tf_op jit(solution)/shard_map/pmax | solution.py:43
  573.9 57.0 %psum.68 = f32[2048]{0:T(1024)S(1)} all-reduce(f32[2048]{0:T(1024)S(1)} %exponential_multiply_fusion), channel_id=1, replica_groups=mesh['dp'=32,'cent'=8] {'dp'}, use_global_device_ids=true, to_apply=%region_24.0 | all-reduce | flops 2048 | bytes 16384 | tf_op jit(solution)/shard_map/psum | solution.py:44
  635.0 4.4 exponential_reduce_fusion
  639.4 39.6 %pmax.55 = f32[1024]{0:T(1024)S(1)} all-reduce(f32[1024]{0:T(1024)S(1)} %add_reduce_fusion), channel_id=1, replica_groups=mesh['dp'=32,'cent'=8] {'cent'}, use_global_device_ids=true, to_apply=%region_26.0 | all-reduce | flops 1024 | bytes 8192 | tf_op jit(solution)/shard_map/pmax | solution.py:33
  679.0 12.4 %psum.69 = f32[1024]{0:T(1024)S(1)} all-reduce(f32[1024]{0:T(1024)S(1)} %exponential_multiply_fusion.3), channel_id=1, replica_groups=mesh['dp'=32,'cent'=8] {'cent'}, use_global_device_ids=true, to_apply=%region_28.0 | all-reduce | flops 1024 | bytes 8192 | tf_op jit(solution)/shard_map/psum | solution.py:34
  692.0 10.4 %fusion.1 = f32[2048,768]{1,0:T(8,128)} fusion(bf16[1024,768]{1,0:T(8,128)(2,1)} %gather_fusion, f32[1024,2048]{1,0:T(8,128)} %get-tuple-element.7, f32[1024]{0:T(1024)S(1)} %add_negate_fusion, f32[2048]{0:T(1024)S(1)} %add_subtract_fusion), kind=kOutput, calls=%fused_computation.38 | convolution fusion | flops 3227516928 | bytes 16265216 | tf_op jit(solution)/shard_map/dot_general | solution.py:49
  702.4 4.3 convert_reduce_fusion
  706.8 61.3 %psum.70 = f32[2048]{0:T(1024)S(1)} all-reduce(f32[2048]{0:T(1024)S(1)} %convert_reduce_fusion), channel_id=1, replica_groups=mesh['dp'=32,'cent'=8] {'dp'}, use_global_device_ids=true, to_apply=%region_30.0 | all-reduce | flops 2048 | bytes 16384 | tf_op jit(solution)/shard_map/psum | solution.py:53
  768.1 112.1 %all-reduce.2.cloned.1.call-done = f32[2048,768]{1,0:T(8,128)} async-done(((f32[2048,768]{1,0:T(8,128)}), f32[2048,768]{1,0:T(8,128)}) %all-reduce.2.cloned.1.call-update) | async-done | bytes 6291472 | tf_op jit(solution)/shard_map/psum | solution.py:53
  (33 shorter events, 15.9 us)
Async XLA Ops:
  7.2 2.6 copy-start
  7.2 83.8 %all-gather.2.cloned.1.call-start = ((), (), s32[]{:S(2)}) async-start(), calls=%async_computation | async-start | bytes 3244032 | tf_op jit(solution)/shard_map/all_gather | solution.py:22
  9.0 871.3 %all-reduce.2.cloned.1.call-start = ((), (), s32[]{:S(2)}) async-start(), calls=%async_computation.1 | async-start | bytes 12582912 | tf_op jit(solution)/shard_map/psum | solution.py:53
  691.4 0.6 copy-start.3
  702.4 177.9 %copy-start.1 = (f32[64,768]{1,0:T(8,128)S(1)}, f32[64,768]{1,0:T(8,128)}, u32[]{:S(2)}) copy-start(f32[64,768]{1,0:T(8,128)} %param.7) | copy-start | bytes 589828
  702.4 177.9 %copy-start.2 = (f32[64,768]{1,0:T(8,128)S(1)}, f32[64,768]{1,0:T(8,128)}, u32[]{:S(2)}) copy-start(f32[64,768]{1,0:T(8,128)} %param.8) | copy-start | bytes 589828
Sparse Core Ops, SparseCore 0:
  11.2 79.7 all-gather.1
  702.5 177.6 all-reduce.1
where the time goes:
time: 890 us; the launch traced here: 889 us
  blocking collectives  595 us (67%)
  waiting for transfers between devices  188 us (21%)
  other arithmetic  66.1 us (7%)
  matrix products  19.4 us (2%)
  between operations  14.3 us (2%)
    pmax x3, blocking collectives, per_device(): column_overall = lax.pmax(column_highest, 'dp')  177 us
    psum x3, blocking collectives, per_device(): lax.psum(column_summed * jnp.exp(column_highest - column_overall), 'dp')  171 us
    pmax x4, blocking collectives, row_potential(): overall = lax.pmax(highest, 'cent')  136 us
    psum x1, waiting for transfers between devices, per_device(): weighted, weight_mass = lax.psum((weighted, weight_mass), 'dp')  112 us
    all_gather x1, waiting for transfers between devices, per_device(): shard_piece = lax.all_gather(rounded, 'dp', axis=0, tiled=True)  76 us
    psum x1, blocking collectives, per_device(): weighted, weight_mass = lax.psum((weighted, weight_mass), 'dp')  61.3 us
    psum x4, blocking collectives, row_potential(): summed = lax.psum(summed * jnp.exp(highest - overall), 'cent')  49.7 us
  transfers between devices with their start and end apart: 2, of which 2 were waited for; matrix products, arithmetic and copies ran while one was open for 1% of the time, Pallas kernels for 0%

commit v1 on v0

--- a/solution.py
+++ b/solution.py
@@ -41,7 +41,9 @@
         column_highest = jnp.max(column_shifted, axis=0)
         column_summed = jnp.sum(jnp.exp(column_shifted - column_highest[None, :]), axis=0)
         column_overall = lax.pmax(column_highest, "dp")
-        column_summed = lax.psum(column_summed * jnp.exp(column_highest - column_overall), "dp")
+        column_summed = jnp.sum(
+            lax.all_gather(column_summed * jnp.exp(column_highest - column_overall), "dp"), axis=0
+        )
         column_highest = column_overall
         column_pot = balance - (column_highest + jnp.log(column_summed))
     row_pot = row_potential(column_pot)

time: 890 us -> 828 us (0.930)
  blocking collectives: 595 us -> 527 us
    psum x3 -> x0, blocking collectives: 171 us -> none  [per_device(): lax.psum(column_summed * jnp.exp(column_highest - column_overall), 'dp')]
    all_gather x0 -> x3, blocking collectives: none -> 107 us  [per_device(): lax.all_gather(column_summed * jnp.exp(column_highest - column_overall),...]
where the time goes in v1:
time: 828 us; the launch traced here: 827 us
  blocking collectives  527 us (64%)
  waiting for transfers between devices  190 us (23%)
  other arithmetic  68.1 us (8%)
  matrix products  19.4 us (2%)
  between operations  14.2 us (2%)
  local copies, waits for them, and re-layouts  8.42 us (1%)
    pmax x3, blocking collectives, per_device(): column_overall = lax.pmax(column_highest, 'dp')  177 us
    pmax x4, blocking collectives, row_potential(): overall = lax.pmax(highest, 'cent')  131 us
    psum x1, waiting for transfers between devices, per_device(): weighted, weight_mass = lax.psum((weighted, weight_mass), 'dp')  114 us
    all_gather x3, blocking collectives, per_device(): lax.all_gather(column_summed * jnp.exp(column_highest - column_overall),...  107 us
    all_gather x1, waiting for transfers between devices, per_device(): shard_piece = lax.all_gather(rounded, 'dp', axis=0, tiled=True)  76 us
    psum x1, blocking collectives, per_device(): weighted, weight_mass = lax.psum((weighted, weight_mass), 'dp')  61.8 us
    psum x4, blocking collectives, row_potential(): summed = lax.psum(summed * jnp.exp(highest - overall), 'cent')  49.7 us
    reduce_sum x4, other arithmetic, row_potential(): summed = jnp.sum(jnp.exp(shifted - highest[:, None]), axis=1)  17.7 us
  transfers between devices with their start and end apart: 2, of which 2 were waited for; matrix products, arithmetic and copies ran while one was open for 1% of the time, Pallas kernels for 0%

profile of v1, /device:TPU:1, one launch (start us, length us, event | category | flops | bytes accessed | tf_op | source)
XLA Modules:
  0.0 827.2 jit_solution(6818301474034213811)
XLA Ops:
  9.7 5.2 gather_fusion
  15.0 76.0 %all-gather.5.cloned.1.call-done = bf16[2048,768]{1,0:T(8,128)(2,1)} async-done(((bf16[64,768]{1,0:T(8,128)(2,1)}), bf16[2048,768]{1,0:T(8,128)(2,1)}) %all-gather.5.cloned.1.call-update) | async-done | bytes 3145744 | tf_op jit(solution)/shard_map/all_gather | solution.py:22
  93.6 9.1 %fusion.2 = (f32[1024]{0:T(1024)S(1)}, f32[1024,2048]{1,0:T(8,128)}) fusion(f32[2048]{0:T(1024)S(1)} %multiply_reduce_fusion, bf16[1024,768]{1,0:T(8,128)(2,1)} %gather_fusion, bf16[2048,768]{1,0:T(8,128)(2,1)} %all-gather.5.cloned.1.call-done), kind=kOutput, calls=%fused_computation.39 | convolution fusion | flops 3229613056 | bytes 13119488 | tf_op jit(solution)/shard_map/dot_general | solution.py:24
  102.6 16.4 %pmax.49 = f32[1024]{0:T(1024)S(1)} all-reduce(f32[1024]{0:T(1024)S(1)} %get-tuple-element.6), channel_id=1, replica_groups=mesh['dp'=32,'cent'=8] {'cent'}, use_global_device_ids=true, to_apply=%region_2.0 | all-reduce | flops 1024 | bytes 8192 | tf_op jit(solution)/shard_map/pmax | solution.py:33
  119.0 4.6 exponential_reduce_fusion.6
  123.6 12.4 %psum.42 = f32[1024]{0:T(1024)S(1)} all-reduce(f32[1024]{0:T(1024)S(1)} %exponential_multiply_fusion.6), channel_id=1, replica_groups=mesh['dp'=32,'cent'=8] {'cent'}, use_global_device_ids=true, to_apply=%region_4.0 | all-reduce | flops 1024 | bytes 8192 | tf_op jit(solution)/shard_map/psum | solution.py:34
  136.1 4.0 add_reduce_fusion.5
  140.1 4.3 exponential_reduce_fusion.5
  144.4 58.9 %pmax.50 = f32[2048]{0:T(1024)S(1)} all-reduce(f32[2048]{0:T(1024)S(1)} %add_reduce_fusion.5), channel_id=1, replica_groups=mesh['dp'=32,'cent'=8] {'dp'}, use_global_device_ids=true, to_apply=%region_6.0 | all-reduce | flops 2048 | bytes 16384 | tf_op jit(solution)/shard_map/pmax | solution.py:43
  203.3 33.9 %all-gather = f32[65536]{0:T(1024)S(1)} all-gather(f32[2048]{0:T(1024)S(1)} %exponential_multiply_fusion.2), channel_id=2, replica_groups=mesh['dp'=32,'cent'=8] {'dp'}, dimensions={0}, use_global_device_ids=true | all-gather | bytes 270336 | tf_op jit(solution)/shard_map/all_gather | solution.py:45
  238.9 4.0 add_reduce_fusion.4
  243.0 4.4 exponential_reduce_fusion.4
  247.3 38.4 %pmax.51 = f32[1024]{0:T(1024)S(1)} all-reduce(f32[1024]{0:T(1024)S(1)} %add_reduce_fusion.4), channel_id=1, replica_groups=mesh['dp'=32,'cent'=8] {'cent'}, use_global_device_ids=true, to_apply=%region_10.0 | all-reduce | flops 1024 | bytes 8192 | tf_op jit(solution)/shard_map/pmax | solution.py:33
  285.7 12.4 %psum.43 = f32[1024]{0:T(1024)S(1)} all-reduce(f32[1024]{0:T(1024)S(1)} %exponential_multiply_fusion.5), channel_id=1, replica_groups=mesh['dp'=32,'cent'=8] {'cent'}, use_global_device_ids=true, to_apply=%region_12.0 | all-reduce | flops 1024 | bytes 8192 | tf_op jit(solution)/shard_map/psum | solution.py:34
  298.2 4.0 add_reduce_fusion.3
  302.2 4.3 exponential_reduce_fusion.3
  306.5 59.1 %pmax.52 = f32[2048]{0:T(1024)S(1)} all-reduce(f32[2048]{0:T(1024)S(1)} %add_reduce_fusion.3), channel_id=1, replica_groups=mesh['dp'=32,'cent'=8] {'dp'}, use_global_device_ids=true, to_apply=%region_14.0 | all-reduce | flops 2048 | bytes 16384 | tf_op jit(solution)/shard_map/pmax | solution.py:43
  365.6 34.3 %all-gather.1 = f32[65536]{0:T(1024)S(1)} all-gather(f32[2048]{0:T(1024)S(1)} %exponential_multiply_fusion.1), channel_id=3, replica_groups=mesh['dp'=32,'cent'=8] {'dp'}, dimensions={0}, use_global_device_ids=true | all-gather | bytes 270336 | tf_op jit(solution)/shard_map/all_gather | solution.py:45
  401.7 4.0 add_reduce_fusion.2
  405.7 4.4 exponential_reduce_fusion.2
  410.1 38.4 %pmax.53 = f32[1024]{0:T(1024)S(1)} all-reduce(f32[1024]{0:T(1024)S(1)} %add_reduce_fusion.2), channel_id=1, replica_groups=mesh['dp'=32,'cent'=8] {'cent'}, use_global_device_ids=true, to_apply=%region_18.0 | all-reduce | flops 1024 | bytes 8192 | tf_op jit(solution)/shard_map/pmax | solution.py:33
  448.4 12.4 %psum.44 = f32[1024]{0:T(1024)S(1)} all-reduce(f32[1024]{0:T(1024)S(1)} %exponential_multiply_fusion.4), channel_id=1, replica_groups=mesh['dp'=32,'cent'=8] {'cent'}, use_global_device_ids=true, to_apply=%region_20.0 | all-reduce | flops 1024 | bytes 8192 | tf_op jit(solution)/shard_map/psum | solution.py:34
  464.9 4.3 exponential_reduce_fusion.1
  469.2 59.1 %pmax.54 = f32[2048]{0:T(1024)S(1)} all-reduce(f32[2048]{0:T(1024)S(1)} %add_reduce_fusion.1), channel_id=1, replica_groups=mesh['dp'=32,'cent'=8] {'dp'}, use_global_device_ids=true, to_apply=%region_22.0 | all-reduce | flops 2048 | bytes 16384 | tf_op jit(solution)/shard_map/pmax | solution.py:43
  528.3 39.2 %all-gather.2 = f32[65536]{0:T(1024)} all-gather(f32[2048]{0:T(1024)S(1)} %exponential_multiply_fusion), channel_id=4, replica_groups=mesh['dp'=32,'cent'=8] {'dp'}, dimensions={0}, use_global_device_ids=true | all-gather | bytes 270336 | tf_op jit(solution)/shard_map/all_gather | solution.py:45
  572.6 4.4 exponential_reduce_fusion
  577.0 38.1 %pmax.55 = f32[1024]{0:T(1024)S(1)} all-reduce(f32[1024]{0:T(1024)S(1)} %add_reduce_fusion), channel_id=1, replica_groups=mesh['dp'=32,'cent'=8] {'cent'}, use_global_device_ids=true, to_apply=%region_26.0 | all-reduce | flops 1024 | bytes 8192 | tf_op jit(solution)/shard_map/pmax | solution.py:33
  615.1 12.4 %psum.45 = f32[1024]{0:T(1024)S(1)} all-reduce(f32[1024]{0:T(1024)S(1)} %exponential_multiply_fusion.3), channel_id=1, replica_groups=mesh['dp'=32,'cent'=8] {'cent'}, use_global_device_ids=true, to_apply=%region_28.0 | all-reduce | flops 1024 | bytes 8192 | tf_op jit(solution)/shard_map/psum | solution.py:34
  628.1 10.4 %fusion.1 = f32[2048,768]{1,0:T(8,128)} fusion(bf16[1024,768]{1,0:T(8,128)(2,1)} %gather_fusion, f32[1024,2048]{1,0:T(8,128)} %get-tuple-element.7, f32[1024]{0:T(1024)S(1)} %add_negate_fusion, f32[2048]{0:T(1024)S(1)} %add_subtract_fusion), kind=kOutput, calls=%fused_computation.38 | convolution fusion | flops 3227516928 | bytes 16265216 | tf_op jit(solution)/shard_map/dot_general | solution.py:51
  638.5 4.3 convert_reduce_fusion
  642.8 61.8 %psum.46 = f32[2048]{0:T(1024)S(1)} all-reduce(f32[2048]{0:T(1024)S(1)} %convert_reduce_fusion), channel_id=1, replica_groups=mesh['dp'=32,'cent'=8] {'dp'}, use_global_device_ids=true, to_apply=%region_30.0 | all-reduce | flops 2048 | bytes 16384 | tf_op jit(solution)/shard_map/psum | solution.py:55
  704.7 113.7 %all-reduce.2.cloned.1.call-done = f32[2048,768]{1,0:T(8,128)} async-done(((f32[2048,768]{1,0:T(8,128)}), f32[2048,768]{1,0:T(8,128)}) %all-reduce.2.cloned.1.call-update) | async-done | bytes 6291472 | tf_op jit(solution)/shard_map/psum | solution.py:55
  (39 shorter events, 20.4 us)
Async XLA Ops:
  7.2 2.6 copy-start
  7.2 83.8 %all-gather.5.cloned.1.call-start = ((), (), s32[]{:S(2)}) async-start(), calls=%async_computation | async-start | bytes 3244032 | tf_op jit(solution)/shard_map/all_gather | solution.py:22
  9.0 809.4 %all-reduce.2.cloned.1.call-start = ((), (), s32[]{:S(2)}) async-start(), calls=%async_computation.1 | async-start | bytes 12582912 | tf_op jit(solution)/shard_map/psum | solution.py:55
  627.5 0.6 copy-start.3
  638.5 179.9 %copy-start.1 = (f32[64,768]{1,0:T(8,128)S(1)}, f32[64,768]{1,0:T(8,128)}, u32[]{:S(2)}) copy-start(f32[64,768]{1,0:T(8,128)} %param.7) | copy-start | bytes 589828
  638.5 179.9 %copy-start.2 = (f32[64,768]{1,0:T(8,128)S(1)}, f32[64,768]{1,0:T(8,128)}, u32[]{:S(2)}) copy-start(f32[64,768]{1,0:T(8,128)} %param.8) | copy-start | bytes 589828
Sparse Core Ops, SparseCore 0:
  11.2 79.7 all-gather.4
  638.6 179.7 all-reduce.1
